TPU v7x, 1024 devices: a whole 8x8x8 slice. The times are simulated.
1024 devices in a mesh: inner: 64 (over x_hi, z, core), outer: 16 (over x_lo, y).
Axes of the slice: x: 8 (x_hi: 4, x_lo: 2; x = x_hi * 2 + x_lo), y: 8, z: 8, core: 2. Of those that a mesh axis runs over, the one named last changes fastest.
Arguments:
- grads: bfloat16 [16, 64, 1048576], P('outer', 'inner'), may hold values from -1.5 to 1.5, as said below
- master: float32 [1048576], P(('inner', 'outer')), may hold values from -3 to 3
- moment: float32 [1048576], P(('inner', 'outer')), may hold values from -2 to 2
- second: float32 [1048576], P(('inner', 'outer')), may hold values from 0.05 to 2
Outputs:
- params_full: bfloat16 [1048576], P('inner')
- new_master: float32 [1048576], P(('inner', 'outer'))
- new_moment: float32 [1048576], P(('inner', 'outer'))
- new_second: float32 [1048576], P(('inner', 'outer'))
Inputs may be any that keep to these rules, and one draw needn't show every extreme that they name: `grads`: gradient values are real-valued, of magnitude at most 48 / sqrt(1024).
All inputs are finite; a program needn't handle non-finite values.
Results may differ from a plain program's by a relative error of at most 0.015.
Values may be sent and summed in bfloat16 or wider, within the bound.
A program may use at most 32 MiB of HBM per device.

v0:
```python
import jax
import jax.numpy as jnp
from jax import lax
from jax.sharding import PartitionSpec as P

QB = 2048
STEP = 100


beta_one = 0.9
beta_two = 0.95
adam_eps = 1e-08
learn_rate = 0.01
weight_decay = 0.1


def as_sent(x):
    return jax.tree.map(lambda a: a.astype(jnp.bfloat16) if a.dtype == jnp.float32 else a, x)


def quantize(values):
    largest = jnp.max(jnp.abs(values), axis=-1)
    scales = largest + 1e-06
    levels = (values / scales[..., None]).astype(jnp.bfloat16)
    return (levels, scales)


def restore(levels, scales):
    return levels.astype(jnp.float32) * scales[..., None]


def adamw(gradient, master, moment, second):
    new_moment = beta_one * moment + (1.0 - beta_one) * gradient
    new_second = beta_two * second + (1.0 - beta_two) * gradient * gradient
    first_corr = 1.0 - beta_one**STEP
    second_corr = 1.0 - beta_two**STEP
    direction = new_moment / first_corr / (jnp.sqrt(new_second / second_corr) + adam_eps)
    new_master = master - learn_rate * (direction + weight_decay * master)
    return (new_master, new_moment, new_second)


def sum_restore(members):
    return jnp.sum(restore(members[0], members[1]), axis=0)


def per_device(grads, master, moment, second):
    inner_count = lax.axis_size("inner")
    outer_count = lax.axis_size("outer")
    local = grads.reshape(-1)
    total_blocks = local.shape[0] // QB
    per_inner = total_blocks // inner_count
    levels, scales = quantize(local.astype(jnp.float32).reshape(inner_count, per_inner, QB))
    partial_value = sum_restore(
        (
            lax.all_to_all(levels, "inner", split_axis=0, concat_axis=0, tiled=True),
            lax.all_to_all(
                scales.astype(jnp.bfloat16), "inner", split_axis=0, concat_axis=0, tiled=True
            ).astype(scales.dtype),
        )
    )
    share_len = master.shape[0]
    partial_value = partial_value.reshape(outer_count, 1, share_len)
    levels_two, scales_two = quantize(partial_value)
    gradient = sum_restore(
        (
            lax.all_to_all(levels_two, "outer", split_axis=0, concat_axis=0, tiled=True),
            lax.all_to_all(
                as_sent(scales_two), "outer", split_axis=0, concat_axis=0, tiled=True
            ).astype(scales_two.dtype),
        )
    )
    gradient = gradient.reshape(-1)
    new_master, new_moment, new_second = adamw(gradient, master, moment, second)
    fresh = new_master.astype(jnp.bfloat16)
    params_full = lax.all_gather(fresh, "outer", axis=0, tiled=True)
    return (params_full, new_master, new_moment, new_second)


def solution(mesh):
    in_specs = (
        P("outer", "inner", None),
        P(("inner", "outer")),
        P(("inner", "outer")),
        P(("inner", "outer")),
    )
    out_specs = (P("inner"), P(("inner", "outer")), P(("inner", "outer")), P(("inner", "outer")))
    return jax.shard_map(
        per_device, mesh=mesh, in_specs=in_specs, out_specs=out_specs, check_vma=False
    )
```

profile of v0, /device:TPU:14, one launch (start us, length us, event | category | flops | bytes accessed | tf_op | source)
XLA Modules:
  0.0 203.4 jit_solution(15554437686600884145)
XLA Ops:
  0.6 37.8 %convert_reduce_fusion = f32[1048576]{0:T(1024)} fusion(bf16[1,1,1048576]{2,1,0:T(2,128)(2,1)} %param.4), kind=kLoop, calls=%fused_computation | loop fusion | flops 1048576 | bytes 6291456 | tf_op jit(solution)/shard_map/convert_element_type | solution.py:52
  38.4 4.9 %reshape.123 = f32[64,8,2048]{2,1,0:T(8,128)} reshape(f32[1048576]{0:T(1024)} %convert_reduce_fusion) | data formatting | bytes 8388608 | tf_op jit(solution)/shard_map/convert_element_type | solution.py:52
  43.3 2.6 %abs_reduce_fusion = f32[64,8]{1,0:T(8,128)S(1)} fusion(f32[64,8,2048]{2,1,0:T(8,128)} %reshape.123), kind=kLoop, calls=%fused_computation.3 | loop fusion | flops 2096640 | bytes 4196352 | tf_op jit(solution)/shard_map/reduce_max | solution.py:22
  45.9 0.1 copy.15
  45.9 0.7 copy.17
  46.7 22.8 %all-to-all-start.1 = ((bf16[64,1,8]{2,1,0:T(2,128)(2,1)}), bf16[64,1,8]{2,1,0:T(2,128)(2,1)S(1)}, u32[]{:S(2)}, u32[]{:S(2)}) async-start(bf16[64,1,8]{2,1,0:T(2,128)(2,1)} %copy.17), calls=%async_computation.1 | async-start | bytes 65536 | tf_op jit(solution)/shard_map/all_to_all | solution.py:56
  69.4 0.1 copy.16
  69.5 4.1 %divide_convert_fusion = bf16[64,8,2048]{2,1,0:T(8,128)(2,1)} fusion(f32[64,8,2048]{2,1,0:T(8,128)} %reshape.123, f32[64,8]{1,0:T(8,128)S(1)} %copy.16), kind=kLoop, calls=%fused_computation.2 | loop fusion | flops 2097152 | bytes 6293504 | tf_op jit(solution)/shard_map/convert_element_type | solution.py:24
  73.6 0.0 copy-start
  73.6 0.0 copy-start.1
  73.7 0.0 copy-start.2
  73.7 4.2 %all-to-all-done.1 = bf16[64,1,8]{2,1,0:T(2,128)(2,1)S(1)} async-done(((bf16[64,1,8]{2,1,0:T(2,128)(2,1)}), bf16[64,1,8]{2,1,0:T(2,128)(2,1)S(1)}, u32[]{:S(2)}, u32[]{:S(2)}) %all-to-all-start.1) | async-done | bytes 1056 | tf_op jit(solution)/shard_map/all_to_all | solution.py:56
  77.8 8.7 %all-to-all-start = ((bf16[64,8,2048]{2,1,0:T(8,128)(2,1)}), bf16[64,8,2048]{2,1,0:T(8,128)(2,1)S(1)}, u32[]{:S(2)}, u32[]{:S(2)}) async-start(bf16[64,8,2048]{2,1,0:T(8,128)(2,1)} %divide_convert_fusion), calls=%async_computation | async-start | bytes 4194304 | tf_op jit(solution)/shard_map/all_to_all | solution.py:55
  86.6 54.4 %all-to-all-done = bf16[64,8,2048]{2,1,0:T(8,128)(2,1)S(1)} async-done(((bf16[64,8,2048]{2,1,0:T(8,128)(2,1)}), bf16[64,8,2048]{2,1,0:T(8,128)(2,1)S(1)}, u32[]{:S(2)}, u32[]{:S(2)}) %all-to-all-start) | async-done | bytes 2097184 | tf_op jit(solution)/shard_map/all_to_all | solution.py:55
  141.0 0.5 multiply_reduce_fusion
  141.5 0.1 reshape.122
  141.6 0.2 abs_reduce_fusion.1
  141.8 0.1 divide_convert_fusion.1
  141.9 0.7 copy.18
  142.6 9.0 %all-to-all-start.3 = ((bf16[16,1,1]{2,1,0:T(2,128)(2,1)}), bf16[16,1,1]{2,1,0:T(2,128)(2,1)S(1)}, u32[]{:S(2)}, u32[]{:S(2)}) async-start(bf16[16,1,1]{2,1,0:T(2,128)(2,1)} %copy.18), calls=%async_computation.3 | async-start | bytes 16384 | tf_op jit(solution)/shard_map/all_to_all | solution.py:67
  151.7 0.5 broadcast.67
  152.2 0.8 reduce.8
  153.0 0.6 reshape.134
  153.6 5.2 %all-to-all-done.3 = bf16[16,1,1]{2,1,0:T(2,128)(2,1)S(1)} async-done(((bf16[16,1,1]{2,1,0:T(2,128)(2,1)}), bf16[16,1,1]{2,1,0:T(2,128)(2,1)S(1)}, u32[]{:S(2)}, u32[]{:S(2)}) %all-to-all-start.3) | async-done | bytes 64 | tf_op jit(solution)/shard_map/all_to_all | solution.py:67
  158.8 4.6 %all-to-all-start.2 = ((bf16[16,2,512]{2,1,0:T(2,128)(2,1)}), bf16[16,2,512]{2,1,0:T(2,128)(2,1)S(1)}, u32[]{:S(2)}, u32[]{:S(2)}) async-start(bf16[16,2,512]{2,1,0:T(2,128)(2,1)} %reshape.134), calls=%async_computation.2 | async-start | bytes 65536 | tf_op jit(solution)/shard_map/all_to_all | solution.py:66
  163.4 0.2 convert_reduce_fusion.1
  163.6 7.0 %all-to-all-done.2 = bf16[16,2,512]{2,1,0:T(2,128)(2,1)S(1)} async-done(((bf16[16,2,512]{2,1,0:T(2,128)(2,1)}), bf16[16,2,512]{2,1,0:T(2,128)(2,1)S(1)}, u32[]{:S(2)}, u32[]{:S(2)}) %all-to-all-start.2) | async-done | bytes 32800 | tf_op jit(solution)/shard_map/all_to_all | solution.py:66
  170.6 0.1 multiply_reduce_fusion.1
  170.7 0.0 copy-done
  170.7 0.0 copy-done.1
  170.8 0.0 copy-done.2
  170.8 0.6 fusion.1
  171.4 31.4 %all_gather.3 = bf16[16384]{0:T(1024)(128)(2,1)S(1)} all-gather(bf16[1024]{0:T(1024)(128)(2,1)S(1)} %get-tuple-element.4), channel_id=1, replica_groups=mesh['inner'=64,'outer'=16] {'outer'}, dimensions={0}, use_global_device_ids=true | all-gather | bytes 34816 | tf_op jit(solution)/shard_map/all_gather | solution.py:75
  202.8 0.6 copy.20
  (4 shorter events, 0.1 us)
Async XLA Ops:
  46.7 31.2 %all-to-all-start.1 = ((bf16[64,1,8]{2,1,0:T(2,128)(2,1)}), bf16[64,1,8]{2,1,0:T(2,128)(2,1)S(1)}, u32[]{:S(2)}, u32[]{:S(2)}) async-start(bf16[64,1,8]{2,1,0:T(2,128)(2,1)} %copy.17), calls=%async_computation.1 | async-start | bytes 65536 | tf_op jit(solution)/shard_map/all_to_all | solution.py:56
  73.6 97.1 %copy-start = (f32[1024]{0:T(1024)S(1)}, f32[1024]{0:T(1024)}, u32[]{:S(2)}) copy-start(f32[1024]{0:T(1024)} %param.5) | copy-start | bytes 12292
  73.6 97.1 %copy-start.1 = (f32[1024]{0:T(1024)S(1)}, f32[1024]{0:T(1024)}, u32[]{:S(2)}) copy-start(f32[1024]{0:T(1024)} %param.6) | copy-start | bytes 12292
  73.7 97.1 %copy-start.2 = (f32[1024]{0:T(1024)S(1)}, f32[1024]{0:T(1024)}, u32[]{:S(2)}) copy-start(f32[1024]{0:T(1024)} %param.7) | copy-start | bytes 12292
  77.8 63.2 %all-to-all-start = ((bf16[64,8,2048]{2,1,0:T(8,128)(2,1)}), bf16[64,8,2048]{2,1,0:T(8,128)(2,1)S(1)}, u32[]{:S(2)}, u32[]{:S(2)}) async-start(bf16[64,8,2048]{2,1,0:T(8,128)(2,1)} %divide_convert_fusion), calls=%async_computation | async-start | bytes 4194304 | tf_op jit(solution)/shard_map/all_to_all | solution.py:55
  142.6 16.2 %all-to-all-start.3 = ((bf16[16,1,1]{2,1,0:T(2,128)(2,1)}), bf16[16,1,1]{2,1,0:T(2,128)(2,1)S(1)}, u32[]{:S(2)}, u32[]{:S(2)}) async-start(bf16[16,1,1]{2,1,0:T(2,128)(2,1)} %copy.18), calls=%async_computation.3 | async-start | bytes 16384 | tf_op jit(solution)/shard_map/all_to_all | solution.py:67
  158.8 11.8 %all-to-all-start.2 = ((bf16[16,2,512]{2,1,0:T(2,128)(2,1)}), bf16[16,2,512]{2,1,0:T(2,128)(2,1)S(1)}, u32[]{:S(2)}, u32[]{:S(2)}) async-start(bf16[16,2,512]{2,1,0:T(2,128)(2,1)} %reshape.134), calls=%async_computation.2 | async-start | bytes 65536 | tf_op jit(solution)/shard_map/all_to_all | solution.py:66
where the time goes:
time: 204 us; the launch traced here: 203 us
  waiting for transfers between devices  70.8 us (35%)
  other arithmetic  47.1 us (23%)
  starting transfers between devices  45.1 us (22%)
  blocking collectives  31.4 us (15%)
  local copies, waits for them, and re-layouts  8.33 us (4%)
    all_to_all x1, waiting for transfers between devices, per_device(): lax.all_to_all(levels, 'inner', split_axis=0, concat_axis=0, tiled=True)  54.4 us
    convert_element_type x1, other arithmetic, per_device(): local.astype(jnp.float32).reshape(inner_count, per_inner, QB)  37.8 us
    all_gather x1, blocking collectives, per_device(): params_full = lax.all_gather(fresh, 'outer', axis=0, tiled=True)  31.4 us
    all_to_all x1, starting transfers between devices, per_device(): lax.all_to_all(scales.astype(jnp.bfloat16), 'inner', split_axis=0, concat...  22.8 us
    all_to_all x1, starting transfers between devices, per_device(): lax.all_to_all(as_sent(scales_two), 'outer', split_axis=0, concat_axis=0,...  9.03 us
    all_to_all x1, starting transfers between devices, per_device(): lax.all_to_all(levels, 'inner', split_axis=0, concat_axis=0, tiled=True)  8.69 us
    all_to_all x1, waiting for transfers between devices, per_device(): lax.all_to_all(levels_two, 'outer', split_axis=0, concat_axis=0, tiled=True)  6.97 us
    all_to_all x1, waiting for transfers between devices, per_device(): lax.all_to_all(as_sent(scales_two), 'outer', split_axis=0, concat_axis=0,...  5.18 us
  transfers between devices with their start and end apart: 4, of which 4 were waited for; matrix products, arithmetic and copies ran while one was open for 3% of the time, Pallas kernels for 0%

commit v1 on v0

v1 whole, which is shorter than its diff:
```python
import jax
import jax.numpy as jnp
from jax import lax
from jax.experimental import pallas as pl
from jax.experimental.pallas import tpu as pltpu
from jax.sharding import PartitionSpec as P

STEP = 100

beta_one = 0.9
beta_two = 0.95
adam_eps = 1e-08
learn_rate = 0.01
weight_decay = 0.1

MESH = pl.DeviceIdType.MESH
RING = 8
SHARE = 1024
ORDER = (4, 3, 5, 2, 6, 1, 7)


def adamw(gradient, master, moment, second):
    new_moment = beta_one * moment + (1.0 - beta_one) * gradient
    new_second = beta_two * second + (1.0 - beta_two) * gradient * gradient
    first_corr = 1.0 - beta_one**STEP
    second_corr = 1.0 - beta_two**STEP
    direction = new_moment / first_corr / (jnp.sqrt(new_second / second_corr) + adam_eps)
    new_master = master - learn_rate * (direction + weight_decay * master)
    return (new_master, new_moment, new_second)


def kernel(
    grads, master, moment, second,
    params_out, master_out, moment_out, second_out,
    raw, halves, from_core, from_one, part_one, to_two, from_two, part_two, from_three, state, fresh,
    load_sem, state_sem, core_send, core_recv, one_send, one_recv, two_send, two_recv,
    three_send, three_recv, all_send, all_recv,
):
    inner, outer = lax.axis_index("inner"), lax.axis_index("outer")
    x_hi, z, core = inner // 16, (inner // 2) % 8, inner % 2
    x_lo, y = outer // 8, outer % 8
    x = x_hi * 2 + x_lo

    def place(x, y, z, core):
        return ((x // 2) * 16 + z * 2 + core, (x % 2) * 8 + y)

    def along(axis, step):
        cx = lax.rem(x + step, RING) if axis == "x" else x
        cy = lax.rem(y + step, RING) if axis == "y" else y
        cz = lax.rem(z + step, RING) if axis == "z" else z
        return place(cx, cy, cz, core)

    first = jnp.where(core == 0, z, x)
    mate_first = jnp.where(core == 0, x, z)
    second_at = jnp.where(core == 0, y, z)
    third = jnp.where(core == 0, x, y)

    def peer(stage, step):
        on_zero = along(("z", "y", "x")[stage], step)
        on_one = along(("x", "z", "y")[stage], step)
        return tuple(jnp.where(core == 0, a, b) for a, b in zip(on_zero, on_one))

    mate = (inner + 1 - 2 * core, outer)

    parts = 8
    size = grads.shape[-1] // parts
    loads = [
        pltpu.make_async_copy(
            grads.at[:, :, pl.ds(i * size, size)], raw.at[:, :, pl.ds(i * size, size)], load_sem.at[i]
        )
        for i in range(parts)
    ]
    for load in loads:
        load.start()
    state_loads = [
        pltpu.make_async_copy(ref, state.at[i], state_sem.at[i])
        for i, ref in enumerate((master, moment, second))
    ]
    for load in state_loads:
        load.start()

    barrier = pltpu.get_barrier_semaphore()
    count = 0
    for step in ORDER:
        for axis in ("x", "y", "z"):
            pl.semaphore_signal(barrier, inc=1, device_id=along(axis, step), device_id_type=MESH)
            count += 1
    for step in range(1, RING):
        other = (inner, (1 - x_lo) * 8 + lax.rem(y + step, RING))
        pl.semaphore_signal(barrier, inc=1, device_id=other, device_id_type=MESH)
        count += 1
    pl.semaphore_signal(barrier, inc=1, device_id=mate, device_id_type=MESH)
    count += 1

    per_load = 4
    block = SHARE * 16
    for i in range(parts):
        loads[i].wait()

        def pack(j, carry):
            at_hi, at_z = i // 2, (i % 2) * 4 + j
            base = pl.multiple_of(i * size + j * 2 * block, block)
            zero = raw[0, :, pl.ds(base, block)].astype(jnp.float32).reshape(2, 8, 8, 128)
            pair = jnp.concatenate([zero[0], zero[1]], axis=1)
            halves[0, at_z, :, at_hi] = pair.astype(jnp.bfloat16)
            one = raw[0, :, pl.ds(pl.multiple_of(base + block, block), block)]
            one = one.astype(jnp.float32).reshape(2, 4, 16, 128).astype(jnp.bfloat16)
            halves[1, at_hi * 2, at_z] = one[0]
            halves[1, at_hi * 2 + 1, at_z] = one[1]
            return carry

        lax.fori_loop(0, per_load, pack, 0)

    pl.semaphore_wait(barrier, count)

    steps = ORDER + (0,)
    core_copies = []
    for k, step in enumerate(steps):
        copy = pltpu.make_async_remote_copy(
            src_ref=halves.at[1 - core, lax.rem(mate_first + step, RING)],
            dst_ref=from_core.at[k],
            send_sem=core_send.at[k],
            recv_sem=core_recv.at[k],
            device_id=mate,
            device_id_type=MESH,
        )
        copy.start()
        core_copies.append(copy)

    one_copies = []
    for k, step in enumerate(steps):
        core_copies[k].wait_recv()
        at = lax.rem(first + step, RING)
        if step:
            for t in range(8):
                total = halves[core, at, t].astype(jnp.float32) + from_core[k, t].astype(jnp.float32)
                halves[core, at, t] = total.astype(jnp.bfloat16)
            copy = pltpu.make_async_remote_copy(
                src_ref=halves.at[core, at],
                dst_ref=from_one.at[k],
                send_sem=one_send.at[k],
                recv_sem=one_recv.at[k],
                device_id=peer(0, step),
                device_id_type=MESH,
            )
            copy.start()
            one_copies.append(copy)
        else:
            for t in range(8):
                part_one[t] = halves[core, at, t].astype(jnp.float32) + from_core[k, t].astype(jnp.float32)
    for k, step in enumerate(ORDER):
        one_copies[k].wait_recv()
        for t in range(8):
            part_one[t] += from_one[k, t].astype(jnp.float32)

    two_copies = []
    for k, step in enumerate(ORDER):
        to_two[k] = part_one[lax.rem(second_at + step, RING)].astype(jnp.bfloat16)
        copy = pltpu.make_async_remote_copy(
            src_ref=to_two.at[k],
            dst_ref=from_two.at[k],
            send_sem=two_send.at[k],
            recv_sem=two_recv.at[k],
            device_id=peer(1, step),
            device_id_type=MESH,
        )
        copy.start()
        two_copies.append(copy)
    total = part_one[second_at]
    for copy in two_copies[::-1]:
        copy.wait_recv()
    for k in range(len(ORDER)):
        total += from_two[k].astype(jnp.float32)
    part_two[...] = total.reshape(8, 8, 128)

    three_copies = []
    for k, step in enumerate(ORDER):
        copy = pltpu.make_async_remote_copy(
            src_ref=part_two.at[lax.rem(third + step, RING)],
            dst_ref=from_three.at[k],
            send_sem=three_send.at[k],
            recv_sem=three_recv.at[k],
            device_id=peer(2, step),
            device_id_type=MESH,
        )
        copy.start()
        three_copies.append(copy)
    for load in state_loads:
        load.wait()
    gradient = part_two[third]
    for copy in three_copies[::-1]:
        copy.wait_recv()
    for k in range(len(ORDER)):
        gradient += from_three[k]

    new_master, new_moment, new_second = adamw(gradient, state[0], state[1], state[2])
    fresh[outer] = new_master

    all_copies = []
    for step in ORDER + (0,):
        for flip in (1, 0):
            if step or flip:
                k = len(all_copies)
                other = (x_lo + flip - 2 * flip * x_lo) * 8 + lax.rem(y + step, RING)
                copy = pltpu.make_async_remote_copy(
                    src_ref=fresh.at[outer],
                    dst_ref=fresh.at[outer],
                    send_sem=all_send.at[k],
                    recv_sem=all_recv.at[k],
                    device_id=(inner, other),
                    device_id_type=MESH,
                )
                copy.start()
                all_copies.append(copy)
    master_out[...] = new_master
    moment_out[...] = new_moment
    second_out[...] = new_second
    for copies in (core_copies, one_copies, two_copies, three_copies):
        for copy in copies:
            copy.wait_send()
    for copy in all_copies[::-1]:
        copy.wait_recv()
    params_out[...] = fresh[...].reshape(128, 128).astype(jnp.bfloat16)
    for copy in all_copies:
        copy.wait_send()


def per_device(grads, master, moment, second):
    shares = [a.reshape(8, 128) for a in (master, moment, second)]
    bf16, f32 = jnp.bfloat16, jnp.float32
    vmem = pl.BlockSpec(memory_space=pltpu.VMEM)
    hbm = pl.BlockSpec(memory_space=pl.ANY)
    dma = pltpu.SemaphoreType.DMA
    others = len(ORDER)
    params, *outs = pl.pallas_call(
        kernel,
        out_shape=[jax.ShapeDtypeStruct((128, 128), bf16)] + [jax.ShapeDtypeStruct((8, 128), f32)] * 3,
        in_specs=[hbm] * 4,
        out_specs=[vmem] * 4,
        scratch_shapes=[
            pltpu.VMEM(grads.shape, bf16),
            pltpu.VMEM((2, 8, 8, 4, 16, 128), bf16),
            pltpu.VMEM((8, 8, 4, 16, 128), bf16),
            pltpu.VMEM((others, 8, 4, 16, 128), bf16),
            pltpu.VMEM((8, 4, 16, 128), f32),
            pltpu.VMEM((others, 4, 16, 128), bf16),
            pltpu.VMEM((others, 4, 16, 128), bf16),
            pltpu.VMEM((8, 8, 128), f32),
            pltpu.VMEM((others, 8, 128), f32),
            pltpu.VMEM((3, 8, 128), f32),
            pltpu.VMEM((16, 8, 128), f32),
            dma((8,)), dma((3,)),
            dma((8,)), dma((8,)),
            dma((others,)), dma((others,)),
            dma((others,)), dma((others,)),
            dma((others,)), dma((others,)),
            dma((15,)), dma((15,)),
        ],
        compiler_params=pltpu.CompilerParams(
            collective_id=0, has_side_effects=True, vmem_limit_bytes=48 << 20
        ),
    )(grads, *shares)
    return (params.reshape(-1), *(a.reshape(-1) for a in outs))


def solution(mesh):
    in_specs = (
        P("outer", "inner", None),
        P(("inner", "outer")),
        P(("inner", "outer")),
        P(("inner", "outer")),
    )
    out_specs = (P("inner"), P(("inner", "outer")), P(("inner", "outer")), P(("inner", "outer")))
    return jax.shard_map(
        per_device, mesh=mesh, in_specs=in_specs, out_specs=out_specs, check_vma=False
    )
```

time: 204 us -> 60.3 us (0.30)
  the two profiles are of different devices: /device:TPU:14 before, /device:TPU:16 now
where the time goes in v1:
time: 60.3 us; the launch traced here: 60 us
  Pallas kernels  52.7 us (87%)
  local copies, waits for them, and re-layouts  6.64 us (11%)
  between operations  0.65 us (1%)
    pallas_call x1, Pallas kernels, per_device(): pl.pallas_call(kernel, out_shape=[jax.ShapeDtypeStruct((128, 128), bf16)]...  52.7 us
    unnamed x12, local copies, waits for them, and re-layouts  6.64 us

profile of v1, /device:TPU:16, one launch (start us, length us, event | category | flops | bytes accessed | tf_op | source)
XLA Modules:
  0.0 60.0 jit_solution(10239796675249425787)
XLA Ops:
  0.6 0.0 copy-start
  0.6 2.2 %copy-done = bf16[1,1,1048576]{2,1,0:T(2,128)(2,1)S(1)} copy-done((bf16[1,1,1048576]{2,1,0:T(2,128)(2,1)S(1)}, bf16[1,1,1048576]{2,1,0:T(2,128)(2,1)}, u32[]{:S(2)}) %copy-start) | copy-done | bytes 2097176
  2.8 0.0 copy-start.1
  2.8 0.7 %copy-done.1 = f32[1024]{0:T(1024)S(1)} copy-done((f32[1024]{0:T(1024)S(1)}, f32[1024]{0:T(1024)}, u32[]{:S(2)}) %copy-start.1) | copy-done | bytes 4120
  3.5 0.0 copy-start.2
  3.5 0.7 %copy-done.2 = f32[1024]{0:T(1024)S(1)} copy-done((f32[1024]{0:T(1024)S(1)}, f32[1024]{0:T(1024)}, u32[]{:S(2)}) %copy-start.2) | copy-done | bytes 4120
  4.2 0.0 copy-start.3
  4.2 0.7 %copy-done.3 = f32[1024]{0:T(1024)S(1)} copy-done((f32[1024]{0:T(1024)S(1)}, f32[1024]{0:T(1024)}, u32[]{:S(2)}) %copy-start.3) | copy-done | bytes 4120
  4.9 52.7 %shard_map.75 = (bf16[128,128]{1,0:T(8,128)(2,1)S(1)}, f32[8,128]{1,0:T(8,128)S(1)}, f32[8,128]{1,0:T(8,128)S(1)}, f32[8,128]{1,0:T(8,128)S(1)}) custom-call(bf16[1,1,1048576]{2,1,0:T(2,128)(2,1)S(1)} %copy-done, f32[8,128]{1,0:T(8,128)S(1)} %bitcast.8, f32[8,128]{1,0:T(8,128)S(1)} %bitcast.9, f32[8,128]{1,0:T(8,128)S(1)} %bitcast.10), custom_call_target="tpu_custom_call" | custom-call | tf_op jit(solution)/shard_map/pallas_call | solution.py:235
  57.6 0.6 %copy.12 = bf16[16384]{0:T(1024)(128)(2,1)} copy(bf16[16384]{0:T(1024)(128)(2,1)S(1)} %bitcast.7) | data formatting | bytes 65536
  58.2 0.6 copy.13
  58.8 0.6 copy.14
  59.4 0.6 copy.15
Async XLA Ops:
  0.6 2.2 %copy-start = (bf16[1,1,1048576]{2,1,0:T(2,128)(2,1)S(1)}, bf16[1,1,1048576]{2,1,0:T(2,128)(2,1)}, u32[]{:S(2)}) copy-start(bf16[1,1,1048576]{2,1,0:T(2,128)(2,1)} %grads.1) | copy-start | bytes 6291460
  2.8 0.7 %copy-start.1 = (f32[1024]{0:T(1024)S(1)}, f32[1024]{0:T(1024)}, u32[]{:S(2)}) copy-start(f32[1024]{0:T(1024)} %param.5) | copy-start | bytes 12292
  3.5 0.7 %copy-start.2 = (f32[1024]{0:T(1024)S(1)}, f32[1024]{0:T(1024)}, u32[]{:S(2)}) copy-start(f32[1024]{0:T(1024)} %param.6) | copy-start | bytes 12292
  4.2 0.7 %copy-start.3 = (f32[1024]{0:T(1024)S(1)}, f32[1024]{0:T(1024)}, u32[]{:S(2)}) copy-start(f32[1024]{0:T(1024)} %param.7) | copy-start | bytes 12292

commit v2 on v1

v2 whole, which is shorter than its diff:
```python
import jax
import jax.numpy as jnp
from jax import lax
from jax.experimental import pallas as pl
from jax.experimental.pallas import tpu as pltpu
from jax.sharding import PartitionSpec as P

STEP = 100

beta_one = 0.9
beta_two = 0.95
adam_eps = 1e-08
learn_rate = 0.01
weight_decay = 0.1

MESH = pl.DeviceIdType.MESH
VMEM_LIMIT = 60 << 20
RING = 8
SHARE = 1024
ORDER = (4, 3, 5, 2, 6, 1, 7)


def adamw(gradient, master, moment, second):
    new_moment = beta_one * moment + (1.0 - beta_one) * gradient
    new_second = beta_two * second + (1.0 - beta_two) * gradient * gradient
    first_corr = 1.0 - beta_one**STEP
    second_corr = 1.0 - beta_two**STEP
    direction = new_moment / first_corr / (jnp.sqrt(new_second / second_corr) + adam_eps)
    new_master = master - learn_rate * (direction + weight_decay * master)
    return (new_master, new_moment, new_second)


CUT = 5


def kernel(
    grads, master, moment, second, result,
    raw, half_a, half_b, core_a, core_b, from_a, from_b, part_one, to_two, from_two, part_two,
    from_three, state,
    load_sem, state_sem, core_send, core_recv, one_send, one_recv, two_send, two_recv,
    three_send, three_recv, all_send, all_recv,
):
    inner, outer = lax.axis_index("inner"), lax.axis_index("outer")
    x_hi, z, core = inner // 16, (inner // 2) % 8, inner % 2
    x_lo, y = outer // 8, outer % 8
    x = x_hi * 2 + x_lo

    def place(x, y, z):
        return ((x // 2) * 16 + z * 2 + core, (x % 2) * 8 + y)

    def along(axis, step):
        cx = lax.rem(x + step, RING) if axis == "x" else x
        cy = lax.rem(y + step, RING) if axis == "y" else y
        cz = lax.rem(z + step, RING) if axis == "z" else z
        return place(cx, cy, cz)

    def pick(condition, a, b):
        return tuple(jnp.where(condition, p, q) for p, q in zip(a, b))

    zero = core == 0
    near = jnp.where(zero, z, y)
    mate_near = jnp.where(zero, y, z)
    slab = jnp.where(zero, y, z)
    low = slab < CUT
    third = jnp.where(low, x, jnp.where(zero, z, y))

    def peer_a(step):
        return pick(zero, along("z", step), along("y", step))

    def peer_b(step):
        return along("x", step)

    def peer_two(step):
        return pick(zero, along("y", step), along("z", step))

    def peer_three(step):
        return pick(low, along("x", step), pick(zero, along("z", step), along("y", step)))

    mate = (inner + 1 - 2 * core, outer)

    parts = 8
    size = grads.shape[-1] // parts
    loads = [
        pltpu.make_async_copy(
            grads.at[:, :, pl.ds(i * size, size)], raw.at[:, :, pl.ds(i * size, size)], load_sem.at[i]
        )
        for i in range(parts)
    ]
    for load in loads:
        load.start()
    state_loads = [
        pltpu.make_async_copy(ref, state.at[i], state_sem.at[i])
        for i, ref in enumerate((master, moment, second))
    ]
    for load in state_loads:
        load.start()

    barrier = pltpu.get_barrier_semaphore()
    count = 0
    for step in ORDER:
        for axis in ("x", "y", "z"):
            pl.semaphore_signal(barrier, inc=1, device_id=along(axis, step), device_id_type=MESH)
            count += 1
    for step in range(1, RING):
        other = (inner, (1 - x_lo) * 8 + lax.rem(y + step, RING))
        pl.semaphore_signal(barrier, inc=1, device_id=other, device_id_type=MESH)
        count += 1
    pl.semaphore_signal(barrier, inc=1, device_id=mate, device_id_type=MESH)
    count += 1

    block = SHARE * 16

    def piece(at_hi, at_z, at_core):
        base = pl.multiple_of(((at_hi * 8 + at_z) * 2 + at_core) * block, block)
        return raw[0, :, pl.ds(base, block)].astype(jnp.float32).reshape(2, 8, 8, 128)

    def tile(a, b):
        return jnp.concatenate([a, b], axis=-2).astype(jnp.bfloat16)

    for part in range(parts):
        loads[part].wait()
        at_hi = part // 2
        for at_z in range(part % 2 * 4, part % 2 * 4 + 4, 2):
            even, odd = piece(at_hi, at_z, 0), piece(at_hi, at_z + 1, 0)
            half_a[0, at_z, :, at_hi] = tile(even[0, :CUT], even[1, :CUT])
            half_a[0, at_z + 1, :, at_hi] = tile(odd[0, :CUT], odd[1, :CUT])
            for lo in range(2):
                half_b[0, at_hi * 2 + lo, :, at_z // 2] = tile(even[lo, CUT:], odd[lo, CUT:])
            for slab_z in (at_z, at_z + 1):
                values = piece(at_hi, slab_z, 1)
                if slab_z < CUT:
                    half_a[1, :, slab_z, at_hi] = tile(values[0], values[1])
                else:
                    for lo in range(2):
                        half_b[1, at_hi * 2 + lo, slab_z - CUT] = values[lo].reshape(4, 16, 128).astype(jnp.bfloat16)

    pl.semaphore_wait(barrier, count)

    def send(src, dst, send_sem, recv_sem, to):
        copy = pltpu.make_async_remote_copy(
            src_ref=src, dst_ref=dst, send_sem=send_sem, recv_sem=recv_sem, device_id=to, device_id_type=MESH
        )
        copy.start()
        return copy

    steps = ORDER + (0,)
    core_copies = []
    for k, step in enumerate(steps):
        for p, half, arrived, at in ((0, half_a, core_a, mate_near), (1, half_b, core_b, x)):
            core_copies.append(send(
                half.at[1 - core, lax.rem(at + step, RING)], arrived.at[k],
                core_send.at[p, k], core_recv.at[p, k], mate,
            ))

    one_copies = []
    for k, step in enumerate(steps):
        for p, half, arrived, landed, at, peer in (
            (0, half_a, core_a, from_a, near, peer_a),
            (1, half_b, core_b, from_b, x, peer_b),
        ):
            core_copies[2 * k + p].wait_recv()
            at = lax.rem(at + step, RING)
            for t in range(arrived.shape[1]):
                total = half[core, at, t].astype(jnp.float32) + arrived[k, t].astype(jnp.float32)
                if step:
                    half[core, at, t] = total.astype(jnp.bfloat16)
                else:
                    part_one[p * CUT + t] = total
            if step:
                one_copies.append(send(
                    half.at[core, at], landed.at[k], one_send.at[p, k], one_recv.at[p, k], peer(step)
                ))
    for k, step in enumerate(ORDER):
        for p, landed in enumerate((from_a, from_b)):
            one_copies[2 * k + p].wait_recv()
            for t in range(landed.shape[1]):
                part_one[p * CUT + t] += landed[k, t].astype(jnp.float32)

    two_copies = []
    for k, step in enumerate(ORDER):
        to_two[k] = part_one[lax.rem(slab + step, RING)].astype(jnp.bfloat16)
        two_copies.append(send(to_two.at[k], from_two.at[k], two_send.at[k], two_recv.at[k], peer_two(step)))
    total = part_one[slab]
    for copy in two_copies[::-1]:
        copy.wait_recv()
    for k in range(len(ORDER)):
        total += from_two[k].astype(jnp.float32)
    part_two[...] = total.reshape(8, 8, 128)

    three_copies = []
    for k, step in enumerate(ORDER):
        three_copies.append(send(
            part_two.at[lax.rem(third + step, RING)], from_three.at[k],
            three_send.at[k], three_recv.at[k], peer_three(step),
        ))
    for load in state_loads:
        load.wait()
    gradient = part_two[third]
    for copy in three_copies[::-1]:
        copy.wait_recv()
    for k in range(len(ORDER)):
        gradient += from_three[k]

    new_master, new_moment, new_second = adamw(gradient, state[0], state[1], state[2])
    result[outer] = new_master

    all_copies = []
    for step in ORDER + (0,):
        for flip in (1, 0):
            if step or flip:
                k = len(all_copies)
                other = (x_lo + flip - 2 * flip * x_lo) * 8 + lax.rem(y + step, RING)
                all_copies.append(send(
                    result.at[outer], result.at[outer], all_send.at[k], all_recv.at[k], (inner, other)
                ))
    result[16] = new_master
    result[17] = new_moment
    result[18] = new_second
    for copies in (core_copies, one_copies, two_copies, three_copies):
        for copy in copies:
            copy.wait_send()
    for copy in all_copies[::-1]:
        copy.wait_recv()
    for copy in all_copies:
        copy.wait_send()


def finish(result, params_out, master_out, moment_out, second_out):
    params_out[...] = result[:16].reshape(128, 128).astype(jnp.bfloat16)
    master_out[...] = result[16]
    moment_out[...] = result[17]
    second_out[...] = result[18]


def per_device(grads, master, moment, second):
    shares = [a.reshape(8, 128) for a in (master, moment, second)]
    bf16, f32 = jnp.bfloat16, jnp.float32
    vmem = pl.BlockSpec(memory_space=pltpu.VMEM)
    hbm = pl.BlockSpec(memory_space=pl.ANY)
    dma = pltpu.SemaphoreType.DMA
    others = len(ORDER)
    rest = RING - CUT
    result = pl.pallas_call(
        kernel,
        out_shape=jax.ShapeDtypeStruct((19, 8, 128), f32),
        in_specs=[hbm] * 4,
        out_specs=vmem,
        scratch_shapes=[
            pltpu.VMEM(grads.shape, bf16),
            pltpu.VMEM((2, 8, CUT, 4, 16, 128), bf16),
            pltpu.VMEM((2, 8, rest, 4, 16, 128), bf16),
            pltpu.VMEM((8, CUT, 4, 16, 128), bf16),
            pltpu.VMEM((8, rest, 4, 16, 128), bf16),
            pltpu.VMEM((others, CUT, 4, 16, 128), bf16),
            pltpu.VMEM((others, rest, 4, 16, 128), bf16),
            pltpu.VMEM((8, 4, 16, 128), f32),
            pltpu.VMEM((others, 4, 16, 128), bf16),
            pltpu.VMEM((others, 4, 16, 128), bf16),
            pltpu.VMEM((8, 8, 128), f32),
            pltpu.VMEM((others, 8, 128), f32),
            pltpu.VMEM((3, 8, 128), f32),
            dma((8,)), dma((3,)),
            dma((2, 8)), dma((2, 8)),
            dma((2, others)), dma((2, others)),
            dma((others,)), dma((others,)),
            dma((others,)), dma((others,)),
            dma((15,)), dma((15,)),
        ],
        compiler_params=pltpu.CompilerParams(
            collective_id=0, has_side_effects=True, vmem_limit_bytes=VMEM_LIMIT
        ),
    )(grads, *shares)
    params, *outs = pl.pallas_call(
        finish,
        out_shape=[jax.ShapeDtypeStruct((128, 128), bf16)] + [jax.ShapeDtypeStruct((8, 128), f32)] * 3,
        in_specs=[vmem],
        out_specs=[vmem] * 4,
        compiler_params=pltpu.CompilerParams(vmem_limit_bytes=VMEM_LIMIT),
    )(result)
    return (params.reshape(-1), *(a.reshape(-1) for a in outs))


def solution(mesh):
    in_specs = (
        P("outer", "inner", None),
        P(("inner", "outer")),
        P(("inner", "outer")),
        P(("inner", "outer")),
    )
    out_specs = (P("inner"), P(("inner", "outer")), P(("inner", "outer")), P(("inner", "outer")))
    return jax.shard_map(
        per_device, mesh=mesh, in_specs=in_specs, out_specs=out_specs, check_vma=False
    )
```

time: 60.3 us -> 51.9 us (0.86)
  the two profiles are of different devices: /device:TPU:16 before, /device:TPU:1 now
where the time goes in v2:
time: 51.9 us; the launch traced here: 51.7 us
  Pallas kernels  51.1 us (98%)
  between operations  0.64 us (1%)
    pallas_call x1, Pallas kernels, per_device(): pl.pallas_call(kernel, out_shape=jax.ShapeDtypeStruct((19, 8, 128), f32),...  49.6 us
    pallas_call x1, Pallas kernels, per_device(): pl.pallas_call(finish, out_shape=[jax.ShapeDtypeStruct((128, 128), bf16)]...  1.52 us

profile of v2, /device:TPU:1, one launch (start us, length us, event | category | flops | bytes accessed | tf_op | source)
XLA Modules:
  0.0 51.7 jit_solution(10742768283972852565)
XLA Ops:
  0.6 49.6 %shard_map.75.result = f32[19,8,128]{2,1,0:T(8,128)} custom-call(bf16[1,1,1048576]{2,1,0:T(2,128)(2,1)} %grads.1, f32[8,128]{1,0:T(8,128)} %bitcast.7, f32[8,128]{1,0:T(8,128)} %bitcast.8, f32[8,128]{1,0:T(8,128)} %bitcast.9), custom_call_target="tpu_custom_call" | custom-call | tf_op jit(solution)/shard_map/pallas_call | solution.py:243
  50.2 1.5 %shard_map.76 = (bf16[128,128]{1,0:T(8,128)(2,1)}, f32[8,128]{1,0:T(8,128)}, f32[8,128]{1,0:T(8,128)}, f32[8,128]{1,0:T(8,128)}) custom-call(f32[19,8,128]{2,1,0:T(8,128)} %shard_map.75.result), custom_call_target="tpu_custom_call" | custom-call | tf_op jit(solution)/shard_map/pallas_call | solution.py:273

commit v3 on v2

--- a/solution.py
+++ b/solution.py
@@ -14,7 +14,7 @@
 weight_decay = 0.1
 
 MESH = pl.DeviceIdType.MESH
-VMEM_LIMIT = 60 << 20
+VMEM_LIMIT = 32 << 20
 RING = 8
 SHARE = 1024
 ORDER = (4, 3, 5, 2, 6, 1, 7)
@@ -35,10 +35,9 @@
 
 def kernel(
     grads, master, moment, second, result,
-    raw, half_a, half_b, core_a, core_b, from_a, from_b, part_one, to_two, from_two, part_two,
-    from_three, state,
+    raw, half_a, half_b, core_a, core_b, from_a, from_b, part_one, from_two, state,
     load_sem, state_sem, core_send, core_recv, one_send, one_recv, two_send, two_recv,
-    three_send, three_recv, all_send, all_recv,
+    all_send, all_recv, entered,
 ):
     inner, outer = lax.axis_index("inner"), lax.axis_index("outer")
     x_hi, z, core = inner // 16, (inner // 2) % 8, inner % 2
@@ -62,19 +61,13 @@
     mate_near = jnp.where(zero, y, z)
     slab = jnp.where(zero, y, z)
     low = slab < CUT
-    third = jnp.where(low, x, jnp.where(zero, z, y))
+    side = jnp.where(zero, z, y)
 
     def peer_a(step):
         return pick(zero, along("z", step), along("y", step))
 
     def peer_b(step):
         return along("x", step)
-
-    def peer_two(step):
-        return pick(zero, along("y", step), along("z", step))
-
-    def peer_three(step):
-        return pick(low, along("x", step), pick(zero, along("z", step), along("y", step)))
 
     mate = (inner + 1 - 2 * core, outer)
 
@@ -96,17 +89,22 @@
         load.start()
 
     barrier = pltpu.get_barrier_semaphore()
+
+    @pl.when(zero)
+    def _():
+        pl.semaphore_signal(barrier, inc=1, device_id=mate, device_id_type=MESH)
+
     count = 0
     for step in ORDER:
         for axis in ("x", "y", "z"):
-            pl.semaphore_signal(barrier, inc=1, device_id=along(axis, step), device_id_type=MESH)
-            count += 1
-    for step in range(1, RING):
-        other = (inner, (1 - x_lo) * 8 + lax.rem(y + step, RING))
-        pl.semaphore_signal(barrier, inc=1, device_id=other, device_id_type=MESH)
-        count += 1
-    pl.semaphore_signal(barrier, inc=1, device_id=mate, device_id_type=MESH)
-    count += 1
+            to_inner, to_outer = along(axis, step)
+            pl.semaphore_signal(barrier, inc=1, device_id=(to_inner - core, to_outer), device_id_type=MESH)
+            count += 2
+
+    @pl.when(core == 1)
+    def _():
+        pl.semaphore_wait(barrier, 1)
+        pl.semaphore_signal(entered, inc=1, device_id=mate, device_id_type=MESH)
 
     block = SHARE * 16
 
@@ -134,7 +132,9 @@
                     for lo in range(2):
                         half_b[1, at_hi * 2 + lo, slab_z - CUT] = values[lo].reshape(4, 16, 128).astype(jnp.bfloat16)
 
-    pl.semaphore_wait(barrier, count)
+    @pl.when(zero)
+    def _():
+        pl.semaphore_wait(entered, 1)
 
     def send(src, dst, send_sem, recv_sem, to):
         copy = pltpu.make_async_remote_copy(
@@ -151,6 +151,15 @@
                 half.at[1 - core, lax.rem(at + step, RING)], arrived.at[k],
                 core_send.at[p, k], core_recv.at[p, k], mate,
             ))
+
+    @pl.when(zero)
+    def _():
+        pl.semaphore_wait(barrier, count)
+        pl.semaphore_signal(entered, inc=1, device_id=mate, device_id_type=MESH)
+
+    @pl.when(core == 1)
+    def _():
+        pl.semaphore_wait(entered, 1)
 
     one_copies = []
     for k, step in enumerate(steps):
@@ -165,41 +174,52 @@
                 if step:
                     half[core, at, t] = total.astype(jnp.bfloat16)
                 else:
-                    part_one[p * CUT + t] = total
+                    part_one[p * CUT + t] = total.reshape(8, 8, 128)
             if step:
                 one_copies.append(send(
                     half.at[core, at], landed.at[k], one_send.at[p, k], one_recv.at[p, k], peer(step)
                 ))
+    targets = []
+    lines = []
+    for step in range(RING):
+        at_x, at_side = lax.rem(x + step, RING), lax.rem(side + step, RING)
+        lines.append((
+            at_x, (at_x // 2) * 16, (at_x % 2) * 8,
+            at_side, jnp.where(zero, at_side * 2, 0), jnp.where(zero, 0, at_side),
+        ))
+    for far in range(RING):
+        s = lax.rem(slab + far, RING)
+        s_low = s < CUT
+        low_in, low_out = jnp.where(zero, z * 2, s * 2 + 1), jnp.where(zero, s, y)
+        high_in = x_hi * 16 + jnp.where(zero, 0, s * 2 + 1)
+        high_out = x_lo * 8 + jnp.where(zero, s, 0)
+        slot = slab * 8 + jnp.where(s_low, x, side)
+        for step in range(RING):
+            if far or step:
+                at_x, x_in, x_out, at_side, side_in, side_out = lines[step]
+                hops = min(far, RING - far) + min(step, RING - step)
+                targets.append((
+                    hops, s, jnp.where(s_low, at_x, at_side), slot,
+                    jnp.where(s_low, x_in + low_in, side_in + high_in),
+                    jnp.where(s_low, x_out + low_out, side_out + high_out),
+                ))
+    targets.sort(key=lambda target: -target[0])
+
     for k, step in enumerate(ORDER):
         for p, landed in enumerate((from_a, from_b)):
             one_copies[2 * k + p].wait_recv()
             for t in range(landed.shape[1]):
-                part_one[p * CUT + t] += landed[k, t].astype(jnp.float32)
-
-    two_copies = []
-    for k, step in enumerate(ORDER):
-        to_two[k] = part_one[lax.rem(slab + step, RING)].astype(jnp.bfloat16)
-        two_copies.append(send(to_two.at[k], from_two.at[k], two_send.at[k], two_recv.at[k], peer_two(step)))
-    total = part_one[slab]
-    for copy in two_copies[::-1]:
-        copy.wait_recv()
-    for k in range(len(ORDER)):
-        total += from_two[k].astype(jnp.float32)
-    part_two[...] = total.reshape(8, 8, 128)
-
-    three_copies = []
-    for k, step in enumerate(ORDER):
-        three_copies.append(send(
-            part_two.at[lax.rem(third + step, RING)], from_three.at[k],
-            three_send.at[k], three_recv.at[k], peer_three(step),
-        ))
+                part_one[p * CUT + t] += landed[k, t].astype(jnp.float32).reshape(8, 8, 128)
+
+    for _, at_slab, at, slot, to_inner, to_outer in targets:
+        send(part_one.at[at_slab, at], from_two.at[slot], two_send, two_recv, (to_inner, to_outer))
+    third = jnp.where(low, x, side)
+    from_two[slab * 8 + third] = part_one[slab, third]
     for load in state_loads:
         load.wait()
-    gradient = part_two[third]
-    for copy in three_copies[::-1]:
-        copy.wait_recv()
-    for k in range(len(ORDER)):
-        gradient += from_three[k]
+    arrived = from_two.at[pl.ds(0, RING * RING - 1)]
+    pltpu.make_async_copy(arrived, arrived, two_recv).wait()
+    gradient = jnp.sum(from_two[...], axis=0)
 
     new_master, new_moment, new_second = adamw(gradient, state[0], state[1], state[2])
     result[outer] = new_master
@@ -216,9 +236,10 @@
     result[16] = new_master
     result[17] = new_moment
     result[18] = new_second
-    for copies in (core_copies, one_copies, two_copies, three_copies):
+    for copies in (core_copies, one_copies):
         for copy in copies:
             copy.wait_send()
+    pltpu.make_async_copy(arrived, arrived, two_send).wait()
     for copy in all_copies[::-1]:
         copy.wait_recv()
     for copy in all_copies:
@@ -253,23 +274,20 @@
             pltpu.VMEM((8, rest, 4, 16, 128), bf16),
             pltpu.VMEM((others, CUT, 4, 16, 128), bf16),
             pltpu.VMEM((others, rest, 4, 16, 128), bf16),
-            pltpu.VMEM((8, 4, 16, 128), f32),
-            pltpu.VMEM((others, 4, 16, 128), bf16),
-            pltpu.VMEM((others, 4, 16, 128), bf16),
-            pltpu.VMEM((8, 8, 128), f32),
-            pltpu.VMEM((others, 8, 128), f32),
+            pltpu.VMEM((8, 8, 8, 128), f32),
+            pltpu.VMEM((64, 8, 128), f32),
             pltpu.VMEM((3, 8, 128), f32),
             dma((8,)), dma((3,)),
             dma((2, 8)), dma((2, 8)),
             dma((2, others)), dma((2, others)),
-            dma((others,)), dma((others,)),
-            dma((others,)), dma((others,)),
+            dma, dma,
             dma((15,)), dma((15,)),
+            pltpu.SemaphoreType.REGULAR,
         ],
         compiler_params=pltpu.CompilerParams(
             collective_id=0, has_side_effects=True, vmem_limit_bytes=VMEM_LIMIT
         ),
-    )(grads, *shares)
+    )(*(pltpu.with_memory_space_constraint(a, pltpu.HBM) for a in (grads, *shares)))
     params, *outs = pl.pallas_call(
         finish,
         out_shape=[jax.ShapeDtypeStruct((128, 128), bf16)] + [jax.ShapeDtypeStruct((8, 128), f32)] * 3,

time: 51.9 us -> 49.2 us (0.948)
  Pallas kernels: 51.1 us -> 48.4 us
    pallas_call x1, Pallas kernels: 49.6 us -> 47.8 us  [per_device(): pl.pallas_call(kernel, out_shape=jax.ShapeDtypeStruct((19, 8, 128), f32),...]
    pallas_call x1, Pallas kernels: 1.52 us -> 0.63 us  [per_device(): pl.pallas_call(finish, out_shape=[jax.ShapeDtypeStruct((128, 128), bf16)]...]
where the time goes in v3:
time: 49.2 us; the launch traced here: 49.1 us
  Pallas kernels  48.4 us (98%)
  between operations  0.64 us (1%)
    pallas_call x1, Pallas kernels, per_device(): pl.pallas_call(kernel, out_shape=jax.ShapeDtypeStruct((19, 8, 128), f32),...  47.8 us

profile of v3, /device:TPU:1, one launch (start us, length us, event | category | flops | bytes accessed | tf_op | source)
XLA Modules:
  0.0 49.1 jit_solution(14628251533359032195)
XLA Ops:
  0.6 47.8 %shard_map.75.result = f32[19,8,128]{2,1,0:T(8,128)S(1)} custom-call(bf16[1,1,1048576]{2,1,0:T(2,128)(2,1)} %grads.1, f32[8,128]{1,0:T(8,128)} %bitcast.7, f32[8,128]{1,0:T(8,128)} %bitcast.8, f32[8,128]{1,0:T(8,128)} %bitcast.9), custom_call_target="tpu_custom_call" | custom-call | tf_op jit(solution)/shard_map/pallas_call | solution.py:264
  48.4 0.6 %shard_map.76 = (bf16[128,128]{1,0:T(8,128)(2,1)}, f32[8,128]{1,0:T(8,128)}, f32[8,128]{1,0:T(8,128)}, f32[8,128]{1,0:T(8,128)}) custom-call(f32[19,8,128]{2,1,0:T(8,128)S(1)} %shard_map.75.result), custom_call_target="tpu_custom_call" | custom-call | tf_op jit(solution)/shard_map/pallas_call | solution.py:291

commit v4 on v3

--- a/solution.py
+++ b/solution.py
@@ -30,6 +30,7 @@
     return (new_master, new_moment, new_second)
 
 
+EARLY = 2
 CUT = 5
 
 
@@ -37,7 +38,7 @@
     grads, master, moment, second, result,
     raw, half_a, half_b, core_a, core_b, from_a, from_b, part_one, from_two, state,
     load_sem, state_sem, core_send, core_recv, one_send, one_recv, two_send, two_recv,
-    all_send, all_recv, entered,
+    all_send, all_recv, entered, known,
 ):
     inner, outer = lax.axis_index("inner"), lax.axis_index("outer")
     x_hi, z, core = inner // 16, (inner // 2) % 8, inner % 2
@@ -57,17 +58,9 @@
         return tuple(jnp.where(condition, p, q) for p, q in zip(a, b))
 
     zero = core == 0
-    near = jnp.where(zero, z, y)
-    mate_near = jnp.where(zero, y, z)
     slab = jnp.where(zero, y, z)
     low = slab < CUT
     side = jnp.where(zero, z, y)
-
-    def peer_a(step):
-        return pick(zero, along("z", step), along("y", step))
-
-    def peer_b(step):
-        return along("x", step)
 
     mate = (inner + 1 - 2 * core, outer)
 
@@ -143,14 +136,22 @@
         copy.start()
         return copy
 
-    steps = ORDER + (0,)
-    core_copies = []
-    for k, step in enumerate(steps):
-        for p, half, arrived, at in ((0, half_a, core_a, mate_near), (1, half_b, core_b, x)):
-            core_copies.append(send(
-                half.at[1 - core, lax.rem(at + step, RING)], arrived.at[k],
-                core_send.at[p, k], core_recv.at[p, k], mate,
-            ))
+    def landed(ref, sem):
+        pltpu.make_async_copy(ref, ref, sem).wait()
+
+    def swap(order):
+        for p, n in order:
+            half, arrived = ((half_a, core_a), (half_b, core_b))[p]
+            send(half.at[1 - core, n], arrived.at[n], core_send.at[p, n], core_recv.at[p, n], mate)
+
+    @pl.when(zero)
+    def _():
+        swap([(0, n) for n in range(RING)] + [(1, n) for n in range(RING)])
+
+    @pl.when(core == 1)
+    def _():
+        early = [(0, n) for n in range(EARLY)] + [(1, n) for n in range(RING)]
+        swap(early + [(0, n) for n in range(EARLY, RING)])
 
     @pl.when(zero)
     def _():
@@ -161,58 +162,148 @@
     def _():
         pl.semaphore_wait(entered, 1)
 
-    one_copies = []
-    for k, step in enumerate(steps):
-        for p, half, arrived, landed, at, peer in (
-            (0, half_a, core_a, from_a, near, peer_a),
-            (1, half_b, core_b, from_b, x, peer_b),
-        ):
-            core_copies[2 * k + p].wait_recv()
-            at = lax.rem(at + step, RING)
-            for t in range(arrived.shape[1]):
-                total = half[core, at, t].astype(jnp.float32) + arrived[k, t].astype(jnp.float32)
+    for step in ORDER:
+        for axis in ("x", "z"):
+            pl.semaphore_signal(known, inc=1, device_id=along(axis, step), device_id_type=MESH)
+
+    steps = ORDER + (0,)
+    first, rest = slice(0, EARLY // 2), slice(EARLY // 2, 4)
+
+    def total(half, arrived, c, at, t, pairs=slice(0, 4)):
+        return half[c, at, t, pairs].astype(jnp.float32) + arrived[at, t, pairs].astype(jnp.float32)
+
+    def add_send(p, c, at, step, ts, pairs, row, to):
+        half, arrived, landing = ((half_a, core_a, from_a), (half_b, core_b, from_b))[p]
+        for t in ts:
+            half[c, at, t, pairs] = total(half, arrived, c, at, t, pairs).astype(jnp.bfloat16)
+        rows, columns = pl.ds(ts[0], len(ts)), pl.ds(pairs.start, pairs.stop - pairs.start)
+        send(
+            half.at[c, at, rows, columns], landing.at[step, rows, columns],
+            one_send.at[row, step], one_recv.at[row, step], to,
+        )
+
+    def keep(p, c, at, ts, pairs):
+        half, arrived = ((half_a, core_a), (half_b, core_b))[p]
+        shares = slice(2 * pairs.start, 2 * pairs.stop)
+        for t in ts:
+            value = total(half, arrived, c, at, t, pairs)
+            part_one[p * CUT + t, shares] = value.reshape(-1, 8, 128)
+
+    def take(p, ts, pairs, row):
+        landing = (from_a, from_b)[p]
+        rows, columns = pl.ds(ts[0], len(ts)), pl.ds(pairs.start, pairs.stop - pairs.start)
+        shares = slice(2 * pairs.start, 2 * pairs.stop)
+        for step in ORDER:
+            landed(landing.at[step, rows, columns], one_recv.at[row, step])
+            for t in ts:
+                value = landing[step, t, pairs].astype(jnp.float32)
+                part_one[p * CUT + t, shares] += value.reshape(-1, 8, 128)
+
+    def hand(s, t, own, to):
+        @pl.when(jnp.logical_or(s != slab, t != own))
+        def _():
+            send(part_one.at[s, t], from_two.at[slab * 8 + own], two_send, two_recv, to)
+
+    slabs_a, slabs_b, whole = tuple(range(CUT)), tuple(range(RING - CUT)), slice(0, 4)
+
+    @pl.when(zero)
+    def _():
+        for n in range(EARLY):
+            landed(core_a.at[n], core_recv.at[0, n])
+            step = lax.rem(n - z + RING, RING)
+
+            @pl.when(step != 0)
+            def _():
+                add_send(0, 0, n, step, slabs_a, whole, 0, place(x, y, n))
+
+            @pl.when(step == 0)
+            def _():
+                keep(0, 0, n, slabs_a, whole)
+
+        for step in steps:
+            at = lax.rem(x + step, RING)
+            landed(core_b.at[at], core_recv.at[1, at])
+            if step:
+                add_send(1, 0, at, step, slabs_b, first, 1, along("x", step))
+            else:
+                keep(1, 0, at, slabs_b, first)
+        for step in steps:
+            n = lax.rem(z + step, RING)
+
+            @pl.when(n >= EARLY)
+            def _():
+                landed(core_a.at[n], core_recv.at[0, n])
                 if step:
-                    half[core, at, t] = total.astype(jnp.bfloat16)
+                    add_send(0, 0, n, step, slabs_a, whole, 0, along("z", step))
                 else:
-                    part_one[p * CUT + t] = total.reshape(8, 8, 128)
+                    keep(0, 0, n, slabs_a, whole)
+
+            at = lax.rem(x + step, RING)
             if step:
-                one_copies.append(send(
-                    half.at[core, at], landed.at[k], one_send.at[p, k], one_recv.at[p, k], peer(step)
-                ))
-    targets = []
-    lines = []
-    for step in range(RING):
-        at_x, at_side = lax.rem(x + step, RING), lax.rem(side + step, RING)
-        lines.append((
-            at_x, (at_x // 2) * 16, (at_x % 2) * 8,
-            at_side, jnp.where(zero, at_side * 2, 0), jnp.where(zero, 0, at_side),
-        ))
-    for far in range(RING):
-        s = lax.rem(slab + far, RING)
-        s_low = s < CUT
-        low_in, low_out = jnp.where(zero, z * 2, s * 2 + 1), jnp.where(zero, s, y)
-        high_in = x_hi * 16 + jnp.where(zero, 0, s * 2 + 1)
-        high_out = x_lo * 8 + jnp.where(zero, s, 0)
-        slot = slab * 8 + jnp.where(s_low, x, side)
-        for step in range(RING):
-            if far or step:
-                at_x, x_in, x_out, at_side, side_in, side_out = lines[step]
-                hops = min(far, RING - far) + min(step, RING - step)
-                targets.append((
-                    hops, s, jnp.where(s_low, at_x, at_side), slot,
-                    jnp.where(s_low, x_in + low_in, side_in + high_in),
-                    jnp.where(s_low, x_out + low_out, side_out + high_out),
-                ))
-    targets.sort(key=lambda target: -target[0])
-
-    for k, step in enumerate(ORDER):
-        for p, landed in enumerate((from_a, from_b)):
-            one_copies[2 * k + p].wait_recv()
-            for t in range(landed.shape[1]):
-                part_one[p * CUT + t] += landed[k, t].astype(jnp.float32).reshape(8, 8, 128)
-
-    for _, at_slab, at, slot, to_inner, to_outer in targets:
-        send(part_one.at[at_slab, at], from_two.at[slot], two_send, two_recv, (to_inner, to_outer))
+                add_send(1, 0, at, step, slabs_b, rest, 2, along("x", step))
+            else:
+                keep(1, 0, at, slabs_b, rest)
+
+        def plane_a():
+            take(0, slabs_a, whole, 0)
+            for step in steps:
+                for far in range(CUT):
+                    s, t = lax.rem(slab + far, CUT), lax.rem(x + step, RING)
+                    hand(s, t, x, place(t, s, z))
+
+        def plane_b(low_z, high_z):
+            for far in range(high_z - low_z):
+                for step in range(RING - CUT):
+                    s = CUT + lax.rem(slab + step, RING - CUT)
+                    t = low_z + lax.rem(z + far, high_z - low_z)
+                    hand(s, t, z, place(x, s, t))
+
+        pl.semaphore_wait(known, 2 * len(ORDER))
+        pl.when(z < EARLY)(plane_a)
+        take(1, slabs_b, first, 1)
+        plane_b(0, EARLY)
+        pl.when(z >= EARLY)(plane_a)
+        take(1, slabs_b, rest, 2)
+        plane_b(EARLY, RING)
+
+    @pl.when(core == 1)
+    def _():
+        for step in steps:
+            at = lax.rem(y + step, RING)
+            landed(core_a.at[at], core_recv.at[0, at])
+            if step:
+                add_send(0, 1, at, step, slabs_a[:EARLY], whole, 0, along("y", step))
+            else:
+                keep(0, 1, at, slabs_a[:EARLY], whole)
+        for step in steps:
+            at, at_x = lax.rem(y + step, RING), lax.rem(x + step, RING)
+            landed(core_b.at[at_x], core_recv.at[1, at_x])
+            if step:
+                add_send(1, 1, at_x, step, slabs_b, whole, 1, along("x", step))
+                add_send(0, 1, at, step, slabs_a[EARLY:], whole, 2, along("y", step))
+            else:
+                keep(1, 1, at_x, slabs_b, whole)
+                keep(0, 1, at, slabs_a[EARLY:], whole)
+
+        def plane_a(low_z, high_z):
+            for step in steps:
+                for far in range(high_z - low_z):
+                    s = low_z + lax.rem(slab + far, high_z - low_z)
+                    t = lax.rem(x + step, RING)
+                    hand(s, t, x, place(t, y, s))
+
+        pl.semaphore_wait(known, 2 * len(ORDER))
+        take(0, slabs_a[:EARLY], whole, 0)
+        plane_a(0, EARLY)
+        take(0, slabs_a[EARLY:], whole, 2)
+        plane_a(EARLY, CUT)
+        take(1, slabs_b, whole, 1)
+        for step in steps:
+            for far in range(RING - CUT):
+                s = CUT + lax.rem(slab + far, RING - CUT)
+                t = lax.rem(y + step, RING)
+                hand(s, t, y, place(x, t, s))
+
     third = jnp.where(low, x, side)
     from_two[slab * 8 + third] = part_one[slab, third]
     for load in state_loads:
@@ -236,9 +327,24 @@
     result[16] = new_master
     result[17] = new_moment
     result[18] = new_second
-    for copies in (core_copies, one_copies):
-        for copy in copies:
-            copy.wait_send()
+    for n in range(RING):
+        landed(core_a.at[n], core_send.at[0, n])
+        landed(core_b.at[n], core_send.at[1, n])
+
+    @pl.when(zero)
+    def _():
+        for step in ORDER:
+            landed(from_a.at[step], one_send.at[0, step])
+            landed(from_b.at[step, :, pl.ds(0, EARLY // 2)], one_send.at[1, step])
+            landed(from_b.at[step, :, pl.ds(EARLY // 2, 4 - EARLY // 2)], one_send.at[2, step])
+
+    @pl.when(core == 1)
+    def _():
+        for step in ORDER:
+            landed(from_a.at[step, pl.ds(0, EARLY)], one_send.at[0, step])
+            landed(from_b.at[step], one_send.at[1, step])
+            landed(from_a.at[step, pl.ds(EARLY, CUT - EARLY)], one_send.at[2, step])
+
     pltpu.make_async_copy(arrived, arrived, two_send).wait()
     for copy in all_copies[::-1]:
         copy.wait_recv()
@@ -259,7 +365,6 @@
     vmem = pl.BlockSpec(memory_space=pltpu.VMEM)
     hbm = pl.BlockSpec(memory_space=pl.ANY)
     dma = pltpu.SemaphoreType.DMA
-    others = len(ORDER)
     rest = RING - CUT
     result = pl.pallas_call(
         kernel,
@@ -272,17 +377,17 @@
             pltpu.VMEM((2, 8, rest, 4, 16, 128), bf16),
             pltpu.VMEM((8, CUT, 4, 16, 128), bf16),
             pltpu.VMEM((8, rest, 4, 16, 128), bf16),
-            pltpu.VMEM((others, CUT, 4, 16, 128), bf16),
-            pltpu.VMEM((others, rest, 4, 16, 128), bf16),
+            pltpu.VMEM((8, CUT, 4, 16, 128), bf16),
+            pltpu.VMEM((8, rest, 4, 16, 128), bf16),
             pltpu.VMEM((8, 8, 8, 128), f32),
             pltpu.VMEM((64, 8, 128), f32),
             pltpu.VMEM((3, 8, 128), f32),
             dma((8,)), dma((3,)),
             dma((2, 8)), dma((2, 8)),
-            dma((2, others)), dma((2, others)),
+            dma((3, 8)), dma((3, 8)),
             dma, dma,
             dma((15,)), dma((15,)),
-            pltpu.SemaphoreType.REGULAR,
+            pltpu.SemaphoreType.REGULAR, pltpu.SemaphoreType.REGULAR,
         ],
         compiler_params=pltpu.CompilerParams(
             collective_id=0, has_side_effects=True, vmem_limit_bytes=VMEM_LIMIT

time: 49.2 us -> 47.1 us (0.957)
  the two profiles are of different devices: /device:TPU:1 before, /device:TPU:256 now
where the time goes in v4:
time: 47.1 us; the launch traced here: 46.9 us
  Pallas kernels  46.3 us (98%)
  between operations  0.64 us (1%)
    pallas_call x1, Pallas kernels, per_device(): pl.pallas_call(kernel, out_shape=jax.ShapeDtypeStruct((19, 8, 128), f32),...  45.7 us

profile of v4, /device:TPU:256, one launch (start us, length us, event | category | flops | bytes accessed | tf_op | source)
XLA Modules:
  0.0 46.9 jit_solution(9319326297180767635)
XLA Ops:
  0.6 45.7 %shard_map.75.result = f32[19,8,128]{2,1,0:T(8,128)S(1)} custom-call(bf16[1,1,1048576]{2,1,0:T(2,128)(2,1)} %grads.1, f32[8,128]{1,0:T(8,128)} %bitcast.7, f32[8,128]{1,0:T(8,128)} %bitcast.8, f32[8,128]{1,0:T(8,128)} %bitcast.9), custom_call_target="tpu_custom_call" | custom-call | tf_op jit(solution)/shard_map/pallas_call | solution.py:369
  46.3 0.6 %shard_map.76 = (bf16[128,128]{1,0:T(8,128)(2,1)}, f32[8,128]{1,0:T(8,128)}, f32[8,128]{1,0:T(8,128)}, f32[8,128]{1,0:T(8,128)}) custom-call(f32[19,8,128]{2,1,0:T(8,128)S(1)} %shard_map.75.result), custom_call_target="tpu_custom_call" | custom-call | tf_op jit(solution)/shard_map/pallas_call | solution.py:396
